TPU v7x, 32 devices: a whole 2x2x4 slice. The times are simulated.
32 devices in a mesh: grp: 2 (over y), freq: 4 (over z), shot: 2 (over x), rcv: 2 (over core).
Axes of the slice: x: 2, y: 2, z: 4, core: 2. Of those that a mesh axis runs over, the one named last changes fastest.
Arguments:
- data: bfloat16 [2, 256, 32, 4096], P(None, 'freq', ('grp', 'shot'), 'rcv'), parts along dimension 2, may hold values from -6 to 6
- estimate: bfloat16 [2, 256, 32, 4096], P(None, 'freq', ('grp', 'shot'), 'rcv'), parts along dimension 2, may hold values from -0.09375 to 0.09375
- window_data: bfloat16 [2, 256, 32, 16], P(None, 'freq', ('grp', 'shot')), parts along dimension 2, may hold values from -6 to 6
- wavelet: float32 [2, 512], P(None, ('grp', 'freq')), parts along dimension 1, may hold values from -24 to 24
- positions: int32 [32], P(('grp', 'shot')), parts along dimension 0, may hold values from 0 to 4095
- bins: int32 [512], P('grp'), parts along dimension 0, may hold values from 0 to 399
- threshold: int32 [2], P('grp'), parts along dimension 0, may hold values from 8 to 40
- step: float32 [2], P('grp'), parts along dimension 0, may hold values from 0.25 to 1
Outputs:
- primaries: bfloat16 [1024, 32, 4096], P('freq', ('grp', 'shot'), 'rcv'), parts along dimension 1
There are 2 independent parts, one for each index of `grp`. A program takes and returns all parts, laid end to end along the dimension named above; each array names one. Nothing has to cross between parts.
All inputs are finite; a program needn't handle non-finite values.
Results may differ from a plain program's by a relative error of at most 0.0059.
The roundings to bfloat16 on the way count: a program that leaves them out, or rounds other values in their place, can miss the bound.
Values may be sent and summed in bfloat16 or wider, within the bound.
A program may use at most 64 MiB of HBM per device.

v0:
```python
from functools import partial
import math
import jax
import jax.numpy as jnp
from jax import lax
from jax.sharding import PartitionSpec as P

NF = 256
RCV = 4096
NT = 1024


def make_down(lines, spots, wavelet, offset):
    width = lines.shape[3]
    columns = offset + lax.iota(jnp.int32, width)
    select = (columns[None, None, :] == spots[None, :, None]).astype(jnp.float32)
    down_re = (wavelet[0][:, None, None] * select - lines[0].astype(jnp.float32)).astype(
        jnp.bfloat16
    )
    down_im = (wavelet[1][:, None, None] * select - lines[1].astype(jnp.float32)).astype(
        jnp.bfloat16
    )
    return (down_re, down_im)


def body(data, estimate, window_data, wavelet, positions, bins, threshold, step):
    product = partial(jnp.einsum, preferred_element_type=jnp.float32)
    offset = lax.axis_index("rcv") * data.shape[3]
    shots_all = data.shape[2] * lax.axis_size("shot")
    norm = 1.0 / math.sqrt(shots_all * RCV)
    lines, spots = (
        lax.all_gather(data, "shot", axis=2, tiled=True),
        lax.all_gather(positions, "shot", axis=0, tiled=True),
    )
    down_re, down_im = make_down(lines, spots, wavelet, offset)
    rows_re = estimate[0]
    rows_im = estimate[1]
    model_re = product("frc,fsc->frs", rows_re, down_re) - product("frc,fsc->frs", rows_im, down_im)
    model_im = product("frc,fsc->frs", rows_re, down_im) + product("frc,fsc->frs", rows_im, down_re)
    model_re, model_im = lax.psum((model_re, model_im), "rcv")
    err_re = (window_data[0].astype(jnp.float32) - model_re).astype(jnp.bfloat16)
    err_im = (window_data[1].astype(jnp.float32) - model_im).astype(jnp.bfloat16)
    grad_re = product("frs,fsc->frc", err_re, down_re) + product("frs,fsc->frc", err_im, down_im)
    grad_im = product("frs,fsc->frc", err_im, down_re) - product("frs,fsc->frc", err_re, down_im)
    step_size = step[0]
    upd_re = (estimate[0].astype(jnp.float32) - step_size * (grad_re * norm)).astype(jnp.bfloat16)
    upd_im = (estimate[1].astype(jnp.float32) - step_size * (grad_im * norm)).astype(jnp.bfloat16)
    updated = jnp.stack([upd_re, upd_im], axis=0)
    n_freq = bins.shape[0]
    times = lax.iota(jnp.int32, NT)
    phase = bins[:, None] * times[None, :] % NT
    angle = 2.0 * math.pi / NT * phase.astype(jnp.float32)
    table = jnp.concatenate([jnp.cos(angle), -jnp.sin(angle)], axis=0).astype(jnp.bfloat16)
    level = threshold[0].astype(jnp.float32) / 64.0
    amplitude = math.sqrt(RCV / NF)
    piece = lax.all_to_all(updated, "freq", split_axis=3, concat_axis=1, tiled=True)
    row_count = piece.shape[2]
    col_count = piece.shape[3]
    stacked = piece.reshape(2 * n_freq, row_count * col_count)
    trace = (
        lax.dot_general(
            table, stacked, (((0,), (0,)), ((), ())), preferred_element_type=jnp.float32
        )
        * amplitude
    )
    sparse = (jnp.sign(trace) * jnp.maximum(jnp.abs(trace) - level, 0.0)).astype(jnp.bfloat16)
    sparse = sparse.reshape(NT, row_count, col_count)
    return lax.all_to_all(sparse, "freq", split_axis=0, concat_axis=2, tiled=True)


def solution(mesh):
    return jax.shard_map(
        body,
        mesh=mesh,
        in_specs=(
            P(None, "freq", ("grp", "shot"), "rcv"),
            P(None, "freq", ("grp", "shot"), "rcv"),
            P(None, "freq", ("grp", "shot"), None),
            P(None, ("grp", "freq")),
            P(("grp", "shot")),
            P("grp"),
            P("grp"),
            P("grp"),
        ),
        out_specs=P("freq", ("grp", "shot"), "rcv"),
        check_vma=False,
    )
```

profile of v0, /device:TPU:0, one launch (start us, length us, event | category | flops | bytes accessed | tf_op | source)
XLA Modules:
  0.0 535.6 jit_solution(10995999869594317697)
XLA Ops:
  8.8 5.2 all-reduce
  14.1 101.5 %all-gather.2.cloned.1.call-done = bf16[2,64,16,2048]{3,2,1,0:T(8,128)(2,1)} async-done(((bf16[2,64,8,2048]{3,2,1,0:T(8,128)(2,1)}), bf16[2,64,16,2048]{3,2,1,0:T(8,128)(2,1)}) %all-gather.2.cloned.1.call-update) | async-done | bytes 8388624 | tf_op jit(solution)/shard_map/all_gather | solution.py:32
  115.6 5.3 fusion
  121.0 1.6 fusion.6
  122.6 1.6 fusion.4
  124.1 2.3 fusion.19
  126.4 1.9 fusion.25
  129.3 18.0 %all-reduce.4.cloned.1.call-done = (f32[64,8,16]{2,1,0:T(8,128)}, f32[64,8,16]{2,1,0:T(8,128)}) async-done(((f32[64,8,16]{2,1,0:T(8,128)}, f32[64,8,16]{2,1,0:T(8,128)}), (f32[64,8,16]{2,1,0:T(8,128)}, f32[64,8,16]{2,1,0:T(8,128)})) %all-reduce.4.cloned.1.call-update) | async-done | bytes 65552 | tf_op jit(solution)/shard_map/psum | solution.py:40
  147.3 3.1 fusion.41
  151.6 1.5 copy-done.1
  153.1 1.3 copy-done.5
  156.3 2.3 pad_maximum_fusion
  158.6 13.2 %copy.23 = bf16[2,64,8,2048]{1,2,0,3:T(8,128)(2,1)} copy(bf16[2,64,8,2048]{3,2,1,0:T(8,128)(2,1)} %pad_maximum_fusion) | data formatting | bytes 8388608 | tf_op jit(solution)/shard_map/stack | solution.py:48
  171.8 9.6 %reshape.71 = bf16[4,2,262144]{2,1,0:T(2,128)(2,1)} reshape(bf16[2048,2,8,64]{3,2,1,0:T(8,128)(2,1)} %bitcast.77) | data formatting | bytes 8388608
  181.4 5.0 all-to-all-start
  187.1 4.9 cosine_convert_fusion
  191.9 88.4 %all-to-all-done = bf16[4,2,262144]{2,1,0:T(2,128)(2,1)} async-done(((bf16[4,2,262144]{2,1,0:T(2,128)(2,1)}), bf16[4,2,262144]{2,1,0:T(2,128)(2,1)}, u32[]{:S(2)}, u32[]{:S(2)}) %all-to-all-start) | async-done | bytes 4194336 | tf_op jit(solution)/shard_map/all_to_all | solution.py:56
  280.3 9.3 %reshape.72 = bf16[2048,2,8,64]{3,2,1,0:T(8,128)(2,1)} reshape(bf16[4,2,262144]{2,1,0:T(2,128)(2,1)} %all-to-all-done) | data formatting | bytes 8388608
  289.6 12.0 %copy.24 = bf16[2,64,8,4,512]{4,2,1,3,0:T(8,128)(2,1)} copy(bf16[2,64,8,4,512]{1,2,0,4,3:T(8,128)(2,1)} %bitcast.78) | data formatting | bytes 8388608 | tf_op jit(solution)/shard_map/all_to_all | solution.py:56
  301.6 4.4 copy.28
  306.0 12.1 %multiply_convert_fusion = bf16[1024,4096]{1,0:T(8,128)(2,1)} fusion(bf16[512,4096]{1,0:T(8,128)(2,1)S(1)} %bitcast.83, f32[]{:T(128)} %bitcast.16, bf16[256,1024]{1,0:T(8,128)(2,1)S(1)} %get-tuple-element.12, bf16[256,1024]{1,0:T(8,128)(2,1)S(1)} %get-tuple-element.11), kind=kOutput, calls=%fused_computation | convolution fusion | flops 4326424576 | bytes 13631492 | tf_op jit(solution)/shard_map/dot_general | solution.py:61
  318.1 12.2 %copy.29 = bf16[128,8,8,512]{3,2,1,0:T(8,128)(2,1)} copy(bf16[128,8,8,512]{3,1,2,0:T(8,128)(2,1)} %bitcast.82) | data formatting | bytes 16777216
  330.3 190.4 %all_to_all.33 = bf16[1024,8,512]{2,1,0:T(8,128)(2,1)} all-to-all(bf16[1024,8,512]{2,1,0:T(8,128)(2,1)} %bitcast.79), channel_id=1, replica_groups=mesh['grp'=2,'freq'=4,'shot'=2,'rcv'=2] {'freq'}, dimensions={0} | all-to-all | bytes 16777216 | tf_op jit(solution)/shard_map/all_to_all | solution.py:68
  520.7 8.1 %copy.25 = bf16[4,256,8,512]{3,2,0,1:T(8,128)(2,1)} copy(bf16[4,256,8,512]{3,2,1,0:T(8,128)(2,1)} %bitcast.80) | data formatting | bytes 16777216 | tf_op jit(solution)/shard_map/all_to_all | solution.py:68
  (40 shorter events, 5.1 us)
Async XLA Ops:
  6.5 0.8 copy-start.12
  6.5 2.0 copy-start.11
  6.5 7.5 %copy-start.10 = (f32[2,64]{1,0:T(2,128)S(1)}, f32[2,64]{1,0:T(2,128)}, u32[]{:S(2)}) copy-start(f32[2,64]{1,0:T(2,128)} %param.11) | copy-start | bytes 1540
  6.5 109.1 %all-gather.2.cloned.1.call-start = ((), (), s32[]{:S(2)}) async-start(), calls=%async_computation.2 | async-start | bytes 12582912 | tf_op jit(solution)/shard_map/all_gather | solution.py:32
  7.3 140.1 %all-reduce.4.cloned.1.call-start = ((), (), s32[]{:S(2)}) async-start(), calls=%async_computation.3 | async-start | bytes 1048576 | tf_op jit(solution)/shard_map/psum | solution.py:40
  115.6 5.3 copy-start.4
  121.0 3.2 copy-start.2
  121.0 5.5 %copy-start = (bf16[64,16,2048]{2,1,0:T(8,128)(2,1)}, bf16[64,16,2048]{2,1,0:T(8,128)(2,1)S(1)}, u32[]{:S(2)}) copy-start(bf16[64,16,2048]{2,1,0:T(8,128)(2,1)S(1)} %get-tuple-element.7) | copy-start | bytes 12582916
  126.4 1.9 copy-start.8
  147.3 3.5 copy-start.3
  147.3 3.5 copy-start.7
  150.9 2.2 copy-start.1
  150.9 3.5 copy-start.5
  154.3 1.0 copy-start.6
  181.4 5.7 %copy-start.9 = (s32[256]{0:T(256)S(1)}, s32[256]{0:T(256)}, u32[]{:S(2)}) copy-start(s32[256]{0:T(256)} %param.13) | copy-start | bytes 3076
  181.4 99.0 %all-to-all-start = ((bf16[4,2,262144]{2,1,0:T(2,128)(2,1)}), bf16[4,2,262144]{2,1,0:T(2,128)(2,1)}, u32[]{:S(2)}, u32[]{:S(2)}) async-start(bf16[4,2,262144]{2,1,0:T(2,128)(2,1)} %reshape.71), calls=%async_computation | async-start | bytes 8388608 | tf_op jit(solution)/shard_map/all_to_all | solution.py:56
Sparse Core Ops, SparseCore 0:
  8.9 106.6 all-gather.1
  128.5 18.7 all-reduce.3
where the time goes:
time: 537 us; the launch traced here: 536 us
  waiting for transfers between devices  209 us (39%)
  blocking collectives  196 us (36%)
  local copies, waits for them, and re-layouts  73.1 us (14%)
  matrix products  25.2 us (5%)
  between operations  15.5 us (3%)
  other arithmetic  12.6 us (2%)
    all_to_all x1, blocking collectives, body(): lax.all_to_all(sparse, 'freq', split_axis=0, concat_axis=2, tiled=True)  190 us
    all_gather x1, waiting for transfers between devices, body(): lax.all_gather(data, 'shot', axis=2, tiled=True)  102 us
    all_to_all x1, waiting for transfers between devices, body(): lax.all_to_all(updated, 'freq', split_axis=3, concat_axis=1, tiled=True)  88.4 us
    unnamed x35, local copies, waits for them, and re-layouts  39.8 us
    psum x1, waiting for transfers between devices, body(): model_re, model_im = lax.psum((model_re, model_im), 'rcv')  18 us
    another operation x1, local copies, waits for them, and re-layouts, body(): updated = jnp.stack([upd_re, upd_im], axis=0)  13.2 us
    dot_general x1, matrix products, body(): lax.dot_general(table, stacked, (((0,), (0,)), ((), ())), preferred_eleme...  12.1 us
    all_to_all x1, local copies, waits for them, and re-layouts, body(): lax.all_to_all(updated, 'freq', split_axis=3, concat_axis=1, tiled=True)  12 us
  transfers between devices with their start and end apart: 3, of which 3 were waited for; matrix products, arithmetic and copies ran while one was open for 1% of the time, Pallas kernels for 0%

commit v1 on v0

--- a/solution.py
+++ b/solution.py
@@ -1,3 +1,4 @@
+import functools
 from functools import partial
 import math
 import jax
@@ -8,6 +9,24 @@
 NF = 256
 RCV = 4096
 NT = 1024
+
+
+def take_boxes(xx, bus_axis):
+    latest, then = (lax.axis_size(bus_axis), lax.axis_index(bus_axis))
+    arr_out = xx.shape[3] // latest
+    passed = jnp.roll(xx, -then * arr_out, axis=3)
+    lanes = [lax.slice_in_dim(passed, 0, arr_out, axis=3)]
+    for h in range(1, latest):
+        tile_out = lax.slice_in_dim(passed, h * arr_out, (h + 1) * arr_out, axis=3)
+        lanes.append(
+            lax.ppermute(tile_out, bus_axis, perm=[(k0, (k0 + h) % latest) for k0 in range(latest)])
+        )
+    earlier = jnp.concatenate(lanes[::-1], axis=1)
+    aux = jnp.roll(earlier, (then + 1) * lanes[0].shape[1], axis=1)
+    return aux
+
+
+supply_the_inputs = functools.partial(take_boxes, bus_axis="freq")
 
 
 def make_down(lines, spots, wavelet, offset):
@@ -53,7 +72,7 @@
     table = jnp.concatenate([jnp.cos(angle), -jnp.sin(angle)], axis=0).astype(jnp.bfloat16)
     level = threshold[0].astype(jnp.float32) / 64.0
     amplitude = math.sqrt(RCV / NF)
-    piece = lax.all_to_all(updated, "freq", split_axis=3, concat_axis=1, tiled=True)
+    piece = supply_the_inputs(updated)
     row_count = piece.shape[2]
     col_count = piece.shape[3]
     stacked = piece.reshape(2 * n_freq, row_count * col_count)

time: 537 us -> 490 us (0.912)
  local copies, waits for them, and re-layouts: 73.1 us -> 31.6 us
    all_to_all x1 -> x0, waiting for transfers between devices: 88.4 us -> none  [body(): lax.all_to_all(updated, 'freq', split_axis=3, concat_axis=1, tiled=True)]
    ppermute x0 -> x3, waiting for transfers between devices: none -> 83.9 us  [take_boxes(): lax.ppermute(tile_out, bus_axis, perm=[(k0, (k0 + h) % latest) for k0 in...]
    unnamed x35 -> x44, local copies, waits for them, and re-layouts: 39.8 us -> 21.3 us
    another operation x1 -> x0, local copies, waits for them, and re-layouts: 13.2 us -> none  [body(): updated = jnp.stack([upd_re, upd_im], axis=0)]
    all_to_all x1 -> x0, local copies, waits for them, and re-layouts: 12 us -> none  [body(): lax.all_to_all(updated, 'freq', split_axis=3, concat_axis=1, tiled=True)]
  transfers between devices with their start and end apart: 3 -> 5, of which waited for: 3 -> 4; matrix products, arithmetic and copies ran while one was open for 1% -> 1% of each run, Pallas kernels for 0% -> 0%
where the time goes in v1:
time: 490 us
  waiting for transfers between devices  204 us (42%)
  blocking collectives  196 us (40%)
  local copies, waits for them, and re-layouts  31.6 us (6%)
  matrix products  25.2 us (5%)
  between operations  15.7 us (3%)
  other arithmetic  12.6 us (3%)
    all_to_all x1, blocking collectives, body(): lax.all_to_all(sparse, 'freq', split_axis=0, concat_axis=2, tiled=True)  190 us
    all_gather x1, waiting for transfers between devices, body(): lax.all_gather(data, 'shot', axis=2, tiled=True)  102 us
    ppermute x3, waiting for transfers between devices, take_boxes(): lax.ppermute(tile_out, bus_axis, perm=[(k0, (k0 + h) % latest) for k0 in...  83.9 us
    unnamed x44, local copies, waits for them, and re-layouts  21.3 us
    psum x1, waiting for transfers between devices, body(): model_re, model_im = lax.psum((model_re, model_im), 'rcv')  18 us
    dot_general x1, matrix products, body(): lax.dot_general(table, stacked, (((0,), (0,)), ((), ())), preferred_eleme...  12.1 us
  transfers between devices with their start and end apart: 5, of which 4 were waited for; matrix products, arithmetic and copies ran while one was open for 1% of the time, Pallas kernels for 0%

profile of v1, /device:TPU:0, one launch (start us, length us, event | category | flops | bytes accessed | tf_op | source)
XLA Modules:
  0.0 489.5 jit_solution(1135150081969682364)
XLA Ops:
  8.8 5.2 %all-reduce = s32[16]{0:T(128)S(1)} all-reduce(s32[16]{0:T(128)S(1)} %dynamic-update-slice), channel_id=1, replica_groups=mesh['grp'=2,'freq'=4,'shot'=2,'rcv'=2] {'shot'}, use_global_device_ids=true, to_apply=%add | all-reduce | flops 16 | bytes 128
  14.1 101.5 %all-gather.2.cloned.1.call-done = bf16[2,64,16,2048]{3,2,1,0:T(8,128)(2,1)} async-done(((bf16[2,64,8,2048]{3,2,1,0:T(8,128)(2,1)}), bf16[2,64,16,2048]{3,2,1,0:T(8,128)(2,1)}) %all-gather.2.cloned.1.call-update) | async-done | bytes 8388624 | tf_op jit(solution)/shard_map/all_gather | solution.py:51
  115.6 5.3 %fusion = (bf16[64,16,2048]{2,1,0:T(8,128)(2,1)S(1)}, bf16[64,16,2048]{2,1,0:T(8,128)(2,1)S(1)}) fusion(bf16[2,64,16,2048]{3,2,1,0:T(8,128)(2,1)} %all-gather.2.cloned.1.call-done, f32[64]{0:T(128)S(1)} %get-tuple-element.16, f32[16,2048]{1,0:T(8,128)S(1)} %compare_convert_fusion, f32[64]{0:T(128)S(1)} %get-tuple-element.17), kind=kLoop, calls=%fused_computation.6 | loop fusion | flops 16777216 | bytes 16908800 | tf_op jit(solution)/shard_map/convert_element_type | solution.py:39
  121.0 1.6 fusion.7
  122.6 1.6 fusion.9
  124.1 1.9 fusion.28
  126.1 2.3 fusion.22
  129.4 18.0 %all-reduce.4.cloned.1.call-done = (f32[64,8,16]{2,1,0:T(8,128)}, f32[64,8,16]{2,1,0:T(8,128)}) async-done(((f32[64,8,16]{2,1,0:T(8,128)}, f32[64,8,16]{2,1,0:T(8,128)}), (f32[64,8,16]{2,1,0:T(8,128)}, f32[64,8,16]{2,1,0:T(8,128)})) %all-reduce.4.cloned.1.call-update) | async-done | bytes 65552 | tf_op jit(solution)/shard_map/psum | solution.py:59
  147.3 3.1 fusion.46
  151.6 1.5 copy-done.1
  153.1 1.3 copy-done.7
  156.3 2.4 fusion.3
  158.7 2.0 copy-done.4
  160.7 1.8 fusion.49
  162.5 3.7 collective-permute-start
  166.1 1.0 collective-permute-start.2
  167.8 4.9 cosine_convert_fusion
  172.7 17.3 %collective-permute-done = bf16[2,64,8,512]{3,2,1,0:T(8,128)(2,1)S(1)} collective-permute-done((bf16[2,64,8,512]{3,2,1,0:T(8,128)(2,1)}, bf16[2,64,8,512]{3,2,1,0:T(8,128)(2,1)S(1)}, u32[]{:S(2)}, u32[]{:S(2)}) %collective-permute-start) | collective-permute-done | bytes 1048608 | tf_op jit(solution)/shard_map/ppermute | solution.py:22
  190.1 66.6 %collective-permute-done.1 = bf16[2,64,8,512]{3,2,1,0:T(8,128)(2,1)S(1)} collective-permute-done((bf16[2,64,8,512]{3,2,1,0:T(8,128)(2,1)}, bf16[2,64,8,512]{3,2,1,0:T(8,128)(2,1)S(1)}, u32[]{:S(2)}, u32[]{:S(2)}) %collective-permute-start.1) | collective-permute-done | bytes 1048608 | tf_op jit(solution)/shard_map/ppermute | solution.py:22
  257.7 2.2 copy.14
  259.9 12.1 %multiply_convert_fusion = bf16[1024,4096]{1,0:T(8,128)(2,1)} fusion(bf16[512,4096]{1,0:T(8,128)(2,1)S(1)} %bitcast.77, f32[]{:T(128)} %bitcast.14, bf16[256,1024]{1,0:T(8,128)(2,1)S(1)} %get-tuple-element.15, bf16[256,1024]{1,0:T(8,128)(2,1)S(1)} %get-tuple-element.14), kind=kOutput, calls=%fused_computation | convolution fusion | flops 4326424576 | bytes 13631492 | tf_op jit(solution)/shard_map/dot_general | solution.py:80
  272.0 12.2 %copy.15 = bf16[128,8,8,512]{3,2,1,0:T(8,128)(2,1)} copy(bf16[128,8,8,512]{3,1,2,0:T(8,128)(2,1)} %bitcast.76) | data formatting | bytes 16777216
  284.2 190.4 %all_to_all.18 = bf16[1024,8,512]{2,1,0:T(8,128)(2,1)} all-to-all(bf16[1024,8,512]{2,1,0:T(8,128)(2,1)} %bitcast.73), channel_id=1, replica_groups=mesh['grp'=2,'freq'=4,'shot'=2,'rcv'=2] {'freq'}, dimensions={0} | all-to-all | bytes 16777216 | tf_op jit(solution)/shard_map/all_to_all | solution.py:87
  474.6 8.1 %copy.11 = bf16[4,256,8,512]{3,2,0,1:T(8,128)(2,1)} copy(bf16[4,256,8,512]{3,2,1,0:T(8,128)(2,1)} %bitcast.74) | data formatting | bytes 16777216 | tf_op jit(solution)/shard_map/all_to_all | solution.py:87
  (54 shorter events, 6.0 us)
Async XLA Ops:
  6.5 0.8 copy-start.14
  6.5 2.0 copy-start.13
  6.5 7.5 %copy-start.12 = (f32[2,64]{1,0:T(2,128)S(1)}, f32[2,64]{1,0:T(2,128)}, u32[]{:S(2)}) copy-start(f32[2,64]{1,0:T(2,128)} %param.11) | copy-start | bytes 1540
  6.5 109.1 %all-gather.2.cloned.1.call-start = ((), (), s32[]{:S(2)}) async-start(), calls=%async_computation.1 | async-start | bytes 12582912 | tf_op jit(solution)/shard_map/all_gather | solution.py:51
  7.3 140.1 %all-reduce.4.cloned.1.call-start = ((), (), s32[]{:S(2)}) async-start(), calls=%async_computation.2 | async-start | bytes 1048576 | tf_op jit(solution)/shard_map/psum | solution.py:59
  115.6 5.3 %copy-start.6 = (bf16[2,64,8,2048]{3,2,1,0:T(8,128)(2,1)S(1)}, bf16[2,64,8,2048]{3,2,1,0:T(8,128)(2,1)}, u32[]{:S(2)}) copy-start(bf16[2,64,8,2048]{3,2,1,0:T(8,128)(2,1)} %param.9) | copy-start | bytes 12582916
  121.0 3.2 copy-start
  121.0 5.1 %copy-start.2 = (bf16[64,16,2048]{2,1,0:T(8,128)(2,1)}, bf16[64,16,2048]{2,1,0:T(8,128)(2,1)S(1)}, u32[]{:S(2)}) copy-start(bf16[64,16,2048]{2,1,0:T(8,128)(2,1)S(1)} %get-tuple-element.8) | copy-start | bytes 12582916
  126.1 2.3 copy-start.10
  147.3 3.5 copy-start.3
  147.3 3.5 copy-start.9
  150.9 2.2 copy-start.1
  150.9 3.5 copy-start.7
  154.3 1.0 copy-start.8
  158.7 2.0 copy-start.4
  160.7 7.1 %copy-start.11 = (s32[256]{0:T(256)S(1)}, s32[256]{0:T(256)}, u32[]{:S(2)}) copy-start(s32[256]{0:T(256)} %param.13) | copy-start | bytes 3076
  162.5 27.6 %collective-permute-start = (bf16[2,64,8,512]{3,2,1,0:T(8,128)(2,1)}, bf16[2,64,8,512]{3,2,1,0:T(8,128)(2,1)S(1)}, u32[]{:S(2)}, u32[]{:S(2)}) collective-permute-start(bf16[2,64,8,512]{3,2,1,0:T(8,128)(2,1)} %get-tuple-element.11), channel_id=1, source_target_pairs={{0,12},{4,0},{8,4},{12,8},{1,13},{5,1},{9,5},{13,9},{2,14},{6,2},{... | collective-permute-start | bytes 3145736 | tf_op jit(solution)/shard_map/ppermute | solution.py:22
  166.1 90.6 %collective-permute-start.1 = (bf16[2,64,8,512]{3,2,1,0:T(8,128)(2,1)}, bf16[2,64,8,512]{3,2,1,0:T(8,128)(2,1)S(1)}, u32[]{:S(2)}, u32[]{:S(2)}) collective-permute-start(bf16[2,64,8,512]{3,2,1,0:T(8,128)(2,1)} %get-tuple-element.10), channel_id=1, source_target_pairs={{0,8},{4,12},{8,0},{12,4},{1,9},{5,13},{9,1},{13,5},{2,10},{6,14},... | collective-permute-start | bytes 3145736 | tf_op jit(solution)/shard_map/ppermute | solution.py:22
  166.1 90.7 %collective-permute-start.2 = (bf16[2,64,8,512]{3,2,1,0:T(8,128)(2,1)}, bf16[2,64,8,512]{3,2,1,0:T(8,128)(2,1)S(1)}, u32[]{:S(2)}, u32[]{:S(2)}) collective-permute-start(bf16[2,64,8,512]{3,2,1,0:T(8,128)(2,1)} %get-tuple-element.9), channel_id=1, source_target_pairs={{0,4},{4,8},{8,12},{12,0},{1,5},{5,9},{9,13},{13,1},{2,6},{6,10},{... | collective-permute-start | bytes 3145736 | tf_op jit(solution)/shard_map/ppermute | solution.py:22
  167.8 89.1 %copy-start.5 = (bf16[2,64,8,2048]{3,2,1,0:T(8,128)(2,1)S(1)}, bf16[2,64,8,2048]{3,2,1,0:T(8,128)(2,1)}, u32[]{:S(2)}) copy-start(bf16[2,64,8,2048]{3,2,1,0:T(8,128)(2,1)} %copy-done.4) | copy-start | bytes 12582916
Sparse Core Ops, SparseCore 0:
  8.9 106.6 all-gather.1
  128.5 18.7 all-reduce.3
